TPU v7x, 512 devices: a whole 4x4x16 slice. The times are simulated.
512 devices in a mesh: tile: 32 (over y, x, core), aux: 16 (over z).
Axes of the slice: x: 4, y: 4, z: 16, core: 2. Of those that a mesh axis runs over, the one named last changes fastest.
Arguments:
- amplitudes: bfloat16 [128, 128, 128], P('tile'), may hold values from -6 to 6
- df_factors: bfloat16 [1536, 3072], P('aux'), may hold values from -0.15625 to 0.15625
- out_tiles: int32 [1024], P(('tile', 'aux')), may hold values from 0 to 23
- pair_col: int32 [1024, 16], P(('tile', 'aux')), may hold values from 0 to 23
- pair_amp: int32 [1024, 16], replicated, may hold values from 0 to 127, as said below
Outputs:
- residual: bfloat16 [1024, 128, 128], P(('tile', 'aux'))
Inputs may be any that keep to these rules, and one draw needn't show every extreme that they name: `pair_amp`: among the 32 entries of the output tiles of one device, no owner occurs more than 2 times, and in every device's entries at least one owner occurs exactly 2 times (several may).
All inputs are finite; a program needn't handle non-finite values.
Results may differ from a plain program's by a relative error of at most 0.0049.
Values may be sent and summed in bfloat16 or wider, within the bound.
A program may use at most 128 MiB of HBM per device.

v0:
```python
import jax
import jax.numpy as jnp
from jax import lax
from jax.sharding import PartitionSpec as P


def body(amplitudes, df_factors, out_tiles, pair_col, pair_amp):
    n_tile = lax.axis_size("tile")
    n_aux = lax.axis_size("aux")
    me_tile = lax.axis_index("tile")
    me_aux = lax.axis_index("aux")
    out_count = out_tiles.shape[0]
    pair_count = pair_col.shape[1]
    tile_size = amplitudes.shape[1]
    pair_width = df_factors.shape[1]
    ptiles = pair_width // tile_size
    per_device = out_count * pair_count
    shard_rows = lax.all_gather(df_factors, "aux", axis=0, tiled=True)
    columns = shard_rows.reshape(shard_rows.shape[0], ptiles, tile_size)
    right_side = jnp.take(columns, out_tiles, axis=1)
    assembled = jnp.einsum(
        "qv,qob->ovb", shard_rows, right_side, preferred_element_type=jnp.float32
    )
    gram_rows = assembled.reshape(out_count, ptiles, tile_size, tile_size)
    panels = jnp.take_along_axis(gram_rows, pair_col[:, :, None, None], axis=1).astype(jnp.bfloat16)
    everyone = pair_amp.reshape(n_tile, n_aux, per_device)
    my_lists = lax.dynamic_index_in_dim(everyone, me_aux, 1, keepdims=False)
    own_list = lax.dynamic_index_in_dim(my_lists, me_tile, 0, keepdims=False)
    all_tiles = lax.all_gather(amplitudes, "tile", axis=0, tiled=True)
    picked = jnp.take(all_tiles, own_list, axis=0)
    stacked = picked.reshape(out_count, pair_count, tile_size, tile_size)
    result = jnp.einsum("okac,okcb->oab", stacked, panels, preferred_element_type=jnp.float32)
    return result.astype(jnp.bfloat16)


def solution(mesh):
    in_specs = (
        P("tile", None, None),
        P("aux", None),
        P(("tile", "aux")),
        P(("tile", "aux"), None),
        P(),
    )
    out_specs = P(("tile", "aux"), None, None)
    return jax.shard_map(body, mesh=mesh, in_specs=in_specs, out_specs=out_specs, check_vma=False)
```

profile of v0, /device:TPU:1, one launch (start us, length us, event | category | flops | bytes accessed | tf_op | source)
XLA Modules:
  0.0 227.0 jit_solution(2826224950712772218)
XLA Ops:
  6.5 0.0 all-gather.3.cloned.1.call-start
  6.5 0.7 all-gather.3.cloned.1.call-update
  7.3 0.0 all-gather.5.cloned.1.call-start
  7.3 0.7 all-gather.5.cloned.1.call-update
  8.0 0.7 bitcast_or_fusion
  8.7 0.1 reshape.94
  8.8 1.0 copy.11
  9.8 0.1 reshape.74
  10.0 0.1 squeeze.8
  10.1 0.7 compare_select_fusion.2
  10.8 0.7 compare_and_fusion
  11.4 0.7 compare_and_fusion.1
  12.1 65.5 %all-gather.3.cloned.1.call-done = bf16[128,128,128]{2,1,0:T(8,128)(2,1)} async-done(((bf16[4,128,128]{2,1,0:T(8,128)(2,1)}), bf16[128,128,128]{2,1,0:T(8,128)(2,1)}) %all-gather.3.cloned.1.call-update) | async-done | bytes 4194320 | tf_op jit(solution)/shard_map/all_gather | solution.py:29
  77.6 3.9 %gather_fusion = bf16[32,128,128]{2,1,0:T(8,128)(2,1)} fusion(bf16[128,128,128]{2,1,0:T(8,128)(2,1)} %all-gather.3.cloned.1.call-done, s32[1024]{0:T(1024)S(1)} %pad_clamp_fusion.1), kind=kCustom, calls=%fused_computation | custom fusion | bytes 2097280 | tf_op jit(solution)/shard_map/jit(_take)/gather | solution.py:30
  81.5 113.8 %all-gather.5.cloned.1.call-done = bf16[1536,3072]{1,0:T(8,128)(2,1)} async-done(((bf16[96,3072]{1,0:T(8,128)(2,1)}), bf16[1536,3072]{1,0:T(8,128)(2,1)}) %all-gather.5.cloned.1.call-update) | async-done | bytes 9437200 | tf_op jit(solution)/shard_map/all_gather | solution.py:18
  195.3 9.9 %copy_bitcast_fusion = bf16[1536,24,128]{2,0,1:T(8,128)(2,1)} fusion(bf16[1536,3072]{1,0:T(8,128)(2,1)} %all-gather.5.cloned.1.call-done), kind=kLoop, calls=%fused_computation.3 | loop fusion | bytes 18874368 | tf_op jit(solution)/shard_map/reshape | solution.py:19
  205.2 4.4 %gather_fusion.1 = bf16[2,1536,128]{2,1,0:T(8,128)(2,1)S(1)} fusion(bf16[1536,24,128]{2,0,1:T(8,128)(2,1)} %copy_bitcast_fusion, s32[1024]{0:T(1024)S(1)} %pad_clamp_fusion), kind=kCustom, calls=%fused_computation.1 | custom fusion | bytes 1572872 | tf_op jit(solution)/shard_map/jit(_take)/gather | solution.py:20
  209.6 6.5 %fusion.2 = bf16[2,3072,128]{1,2,0:T(8,128)(2,1)S(1)} fusion(bf16[1536,3072]{1,0:T(8,128)(2,1)} %all-gather.5.cloned.1.call-done, bf16[2,1536,128]{2,1,0:T(8,128)(2,1)S(1)} %gather_fusion.1, pred[2]{0:T(512)(128)(4,1)S(1)} %compare_and_fusion), kind=kOutput, calls=%fused_computation.6 | convolution fusion | flops 2416312320 | bytes 11796482 | tf_op jit(solution)/shard_map/qv,qob->ovb/dot_general | solution.py:21
  216.1 0.9 copy.17
  217.0 0.8 gather_fusion.2
  217.8 2.4 %fusion.5 = bf16[2,128,128]{2,1,0:T(8,128)(2,1)} fusion(bf16[2,16,128,128]{3,2,1,0:T(8,128)(2,1)S(1)} %bitcast.33, bf16[2,16,128,128]{3,2,1,0:T(8,128)(2,1)} %bitcast.32, pred[2,16]{1,0:T(4,128)(4,1)S(1)} %get-tuple-element.5, pred[2,16]{1,0:T(4,128)(4,1)S(1)} %get-tuple-element.6), kind=kOutput, calls=%fused_computation.9 | convolution fusion | flops 135299072 | bytes 2162752 | tf_op jit(solution)/shard_map/okac,okcb->oab/dot_general | solution.py:32
  (4 shorter events, 0.0 us)
Async XLA Ops:
  6.5 71.1 %all-gather.3.cloned.1.call-start = ((), (), s32[]{:S(2)}) async-start(), calls=%async_computation | async-start | bytes 4325376 | tf_op jit(solution)/shard_map/all_gather | solution.py:29
  7.3 188.0 %all-gather.5.cloned.1.call-start = ((), (), s32[]{:S(2)}) async-start(), calls=%async_computation.1 | async-start | bytes 10027008 | tf_op jit(solution)/shard_map/all_gather | solution.py:18
Sparse Core Ops, SparseCore 0:
  10.5 67.0 all-gather.2
  79.7 115.5 all-gather.4
where the time goes:
time: 227 us
  waiting for transfers between devices  181 us (80%)
  local copies, waits for them, and re-layouts  21.2 us (9%)
  between operations  13.5 us (6%)
  matrix products  8.9 us (4%)
  other arithmetic  2.72 us (1%)
    all_gather x1, waiting for transfers between devices, body(): shard_rows = lax.all_gather(df_factors, 'aux', axis=0, tiled=True)  114 us
    all_gather x1, waiting for transfers between devices, body(): all_tiles = lax.all_gather(amplitudes, 'tile', axis=0, tiled=True)  65.5 us
    reshape x1, local copies, waits for them, and re-layouts, body(): columns = shard_rows.reshape(shard_rows.shape[0], ptiles, tile_size)  9.91 us
    dot_general x1, matrix products, body(): jnp.einsum('qv,qob->ovb', shard_rows, right_side, preferred_element_type=...  6.51 us
  transfers between devices with their start and end apart: 2, of which 2 were waited for; matrix products, arithmetic and copies ran while one was open for 3% of the time, Pallas kernels for 0%

commit v1 on v0

--- a/solution.py
+++ b/solution.py
@@ -2,6 +2,13 @@
 import jax.numpy as jnp
 from jax import lax
 from jax.sharding import PartitionSpec as P
+
+
+def gather_over(x, mesh_axis, d):
+    count = lax.axis_size(mesh_axis)
+    parts = jnp.stack([x for _ in range(count)])
+    parts = lax.all_to_all(parts, mesh_axis, split_axis=0, concat_axis=0)
+    return jnp.concatenate(parts, axis=d)
 
 
 def body(amplitudes, df_factors, out_tiles, pair_col, pair_amp):
@@ -15,7 +22,7 @@
     pair_width = df_factors.shape[1]
     ptiles = pair_width // tile_size
     per_device = out_count * pair_count
-    shard_rows = lax.all_gather(df_factors, "aux", axis=0, tiled=True)
+    shard_rows = gather_over(df_factors, "aux", 0)
     columns = shard_rows.reshape(shard_rows.shape[0], ptiles, tile_size)
     right_side = jnp.take(columns, out_tiles, axis=1)
     assembled = jnp.einsum(

time: 227 us -> 477 us (2.10)
  waiting for transfers between devices: 181 us -> 402 us
  starting transfers between devices: 0.04 us -> 16 us
  local copies, waits for them, and re-layouts: 21.2 us -> 35.7 us
    all_to_all x0 -> x1, waiting for transfers between devices: none -> 335 us  [gather_over(): parts = lax.all_to_all(parts, mesh_axis, split_axis=0, concat_axis=0)]
    all_gather x1 -> x0, waiting for transfers between devices: 114 us -> none  [body(): shard_rows = lax.all_gather(df_factors, 'aux', axis=0, tiled=True)]
    all_to_all x0 -> x1, starting transfers between devices: none -> 15.9 us  [gather_over(): parts = lax.all_to_all(parts, mesh_axis, split_axis=0, concat_axis=0)]
    another operation x0 -> x2, local copies, waits for them, and re-layouts: none -> 15.4 us  [the longest x1 9.45 us: body(): columns = shard_rows.reshape(shard_rows.shape[0], ptiles, tile_size)]
    reshape x1 -> x0, local copies, waits for them, and re-layouts: 9.91 us -> none  [body(): columns = shard_rows.reshape(shard_rows.shape[0], ptiles, tile_size)]
    unnamed x1 -> x8, local copies, waits for them, and re-layouts: 1.03 us -> 10 us
  transfers between devices with their start and end apart: 2 -> 2, of which waited for: 2 -> 2; matrix products, arithmetic and copies ran while one was open for 3% -> 1% of each run, Pallas kernels for 0% -> 0%
where the time goes in v1:
time: 477 us; the launch traced here: 476 us
  waiting for transfers between devices  402 us (84%)
  local copies, waits for them, and re-layouts  35.7 us (7%)
  starting transfers between devices  16 us (3%)
  between operations  13.5 us (3%)
  matrix products  8.89 us (2%)
    all_to_all x1, waiting for transfers between devices, gather_over(): parts = lax.all_to_all(parts, mesh_axis, split_axis=0, concat_axis=0)  335 us
    all_gather x1, waiting for transfers between devices, body(): all_tiles = lax.all_gather(amplitudes, 'tile', axis=0, tiled=True)  65.9 us
    all_to_all x1, starting transfers between devices, gather_over(): parts = lax.all_to_all(parts, mesh_axis, split_axis=0, concat_axis=0)  15.9 us
    unnamed x8, local copies, waits for them, and re-layouts  10 us
  transfers between devices with their start and end apart: 2, of which 2 were waited for; matrix products, arithmetic and copies ran while one was open for 1% of the time, Pallas kernels for 0%

profile of v1, /device:TPU:1, one launch (start us, length us, event | category | flops | bytes accessed | tf_op | source)
XLA Modules:
  0.0 476.0 jit_solution(11721659632497930624)
XLA Ops:
  6.5 5.9 %stack.2 = bf16[16,96,3072]{2,1,0:T(8,128)(2,1)} broadcast(bf16[96,3072]{1,0:T(8,128)(2,1)} %param.6), dimensions={1,2} | broadcast | bytes 10027008 | tf_op jit(solution)/shard_map/stack | solution.py:9
  12.4 0.0 copy-start.1
  12.5 0.0 copy-start
  12.5 0.0 copy-start.2
  12.5 15.9 %all-to-all-start = ((bf16[16,96,3072]{2,1,0:T(8,128)(2,1)}), bf16[16,96,3072]{2,1,0:T(8,128)(2,1)}, u32[]{:S(2)}, u32[]{:S(2)}) async-start(bf16[16,96,3072]{2,1,0:T(8,128)(2,1)} %stack.2), calls=%async_computation | async-start | bytes 18874368 | tf_op jit(solution)/shard_map/all_to_all | solution.py:10
  28.4 0.0 all-gather.2.cloned.1.call-start
  28.4 0.7 all-gather.2.cloned.1.call-update
  29.1 0.0 copy-done.1
  29.1 0.1 reshape.96
  29.2 0.0 copy-done
  29.2 0.2 copy.14
  29.4 0.1 reshape.76
  29.6 0.1 squeeze.8
  29.7 0.0 copy-done.2
  29.8 65.9 %all-gather.2.cloned.1.call-done = bf16[128,128,128]{2,1,0:T(8,128)(2,1)} async-done(((bf16[4,128,128]{2,1,0:T(8,128)(2,1)}), bf16[128,128,128]{2,1,0:T(8,128)(2,1)}) %all-gather.2.cloned.1.call-update) | async-done | bytes 4194320 | tf_op jit(solution)/shard_map/all_gather | solution.py:36
  95.7 3.9 gather_fusion
  99.6 335.3 %all-to-all-done = bf16[16,96,3072]{2,1,0:T(8,128)(2,1)} async-done(((bf16[16,96,3072]{2,1,0:T(8,128)(2,1)}), bf16[16,96,3072]{2,1,0:T(8,128)(2,1)}, u32[]{:S(2)}, u32[]{:S(2)}) %all-to-all-start) | async-done | bytes 9437216 | tf_op jit(solution)/shard_map/all_to_all | solution.py:10
  434.9 9.8 %copy.21 = bf16[192,8,24,128]{3,2,1,0:T(8,128)(2,1)} copy(bf16[192,8,24,128]{3,1,2,0:T(8,128)(2,1)} %bitcast.14) | data formatting | bytes 18874368
  444.7 9.4 %copy.15 = bf16[1536,24,128]{2,0,1:T(8,128)(2,1)} copy(bf16[1536,24,128]{2,1,0:T(8,128)(2,1)} %bitcast.28) | data formatting | bytes 18874368 | tf_op jit(solution)/shard_map/reshape;reshape | solution.py:26
  454.1 4.4 gather_fusion.1
  458.6 6.5 %convolution_bitcast_fusion = bf16[2,3072,128]{1,2,0:T(8,128)(2,1)S(1)} fusion(bf16[1536,3072,1]{1,0,2:T(8,128)(2,1)} %bitcast.5, bf16[2,1536,128]{2,1,0:T(8,128)(2,1)S(1)} %gather_fusion.1, pred[2]{0:T(512)(128)(4,1)S(1)} %compare_and_fusion), kind=kOutput, calls=%fused_computation.3 | convolution fusion | flops 2416312320 | bytes 11796482 | tf_op jit(solution)/shard_map/qv,qob->ovb/dot_general | solution.py:28
  465.1 0.9 copy.20
  466.0 0.8 gather_fusion.2
  466.8 2.4 fusion
  (8 shorter events, 0.1 us)
Async XLA Ops:
  12.4 16.7 %copy-start.1 = (s32[2,16]{1,0:T(2,128)S(1)}, s32[2,16]{1,0:T(2,128)}, u32[]{:S(2)}) copy-start(s32[2,16]{1,0:T(2,128)} %param.8) | copy-start | bytes 388
  12.5 16.8 %copy-start = (s32[1024,16]{0,1:T(8,128)S(1)}, s32[1024,16]{0,1:T(8,128)}, u32[]{:S(2)}) copy-start(s32[1024,16]{0,1:T(8,128)} %param.9) | copy-start | bytes 196612
  12.5 17.3 %copy-start.2 = (s32[2]{0:T(128)S(1)}, s32[2]{0:T(128)}, u32[]{:S(2)}) copy-start(s32[2]{0:T(128)} %param.7) | copy-start | bytes 28
  12.5 422.4 %all-to-all-start = ((bf16[16,96,3072]{2,1,0:T(8,128)(2,1)}), bf16[16,96,3072]{2,1,0:T(8,128)(2,1)}, u32[]{:S(2)}, u32[]{:S(2)}) async-start(bf16[16,96,3072]{2,1,0:T(8,128)(2,1)} %stack.2), calls=%async_computation | async-start | bytes 18874368 | tf_op jit(solution)/shard_map/all_to_all | solution.py:10
  28.4 67.3 %all-gather.2.cloned.1.call-start = ((), (), s32[]{:S(2)}) async-start(), calls=%async_computation.1 | async-start | bytes 4325376 | tf_op jit(solution)/shard_map/all_gather | solution.py:36
Sparse Core Ops, SparseCore 0:
  32.4 63.3 all-gather.1
